TPU v7x, 512 devices: a whole 4x8x8 slice. The times are simulated.
512 devices in a mesh: dp: 32 (over z_lo, y), vocab: 16 (over z_hi, x, core).
Axes of the slice: x: 4, y: 8, z: 8 (z_hi: 2, z_lo: 4; z = z_hi * 4 + z_lo), core: 2. Of those that a mesh axis runs over, the one named last changes fastest.
Arguments:
- hidden_states: bfloat16 [4096, 5120], P('dp'), may hold values from -16 to 16
- positions: int32 [64, 16], P('dp'), may hold values from 0 to 127
- target_ids: int32 [64, 16], replicated, may hold values from 0 to 151551
- head: bfloat16 [151552, 5120], P(('dp', 'vocab')), may hold values from -3 to 3
- out_factor: bfloat16 [151552, 128], P(('dp', 'vocab')), may hold values from -0.5 to 0.5
- in_factor: bfloat16 [5120, 128], P('vocab'), may hold values from -0.0048828125 to 0.0048828125
Outputs:
- gram: float32 [64, 64], P('dp', 'vocab')
All inputs are finite; a program needn't handle non-finite values.
Results may differ from a plain program's by a relative error of at most 0.00078.
Values may be sent and summed in bfloat16 or wider, within the bound.
A program may use at most 64 MiB of HBM per device.

v0:
```python
import jax
import jax.numpy as jnp
from jax import lax
from jax.sharding import PartitionSpec as P

entropy_weight = 0.2


def row_products(left_rows, right_rows):
    return lax.dot_general(
        left_rows, right_rows, (((1,), (1,)), ((), ())), preferred_element_type=jnp.float32
    )


def shards(hidden_states, positions, target_ids, head, out_factor, in_factor):
    sel_count = positions.shape[0]
    token_count = positions.shape[1]
    row_count = sel_count * token_count
    voc_local = head.shape[0]
    rank_full = out_factor.shape[1]
    width_local = in_factor.shape[0]
    vocab_count = lax.axis_size("vocab")
    rank_local = rank_full // vocab_count
    flat_positions = positions.reshape(row_count)
    flat_targets = target_ids.reshape(target_ids.shape[0] * target_ids.shape[1])
    selected = jnp.take(hidden_states, flat_positions, axis=0)
    own_columns = lax.dynamic_slice_in_dim(
        selected, lax.axis_index("vocab") * width_local, width_local, 1
    )
    input_side = lax.psum(
        jnp.dot(own_columns, in_factor, preferred_element_type=jnp.float32), "vocab"
    )
    logits = row_products(lax.all_gather(selected, "dp", axis=0, tiled=True), head)
    total_max = lax.pmax(jnp.max(logits, axis=1), ("dp", "vocab"))
    shifted = jnp.exp(logits - total_max[:, None])
    exp_total, weighted = lax.psum(
        (jnp.sum(shifted, axis=1), jnp.sum(shifted * logits, axis=1)), ("dp", "vocab")
    )
    log_total = total_max + jnp.log(exp_total)
    entropy = log_total - weighted / exp_total
    probs = jnp.exp(logits - log_total[:, None])
    first_vocab = (lax.axis_index("dp") * vocab_count + lax.axis_index("vocab")) * voc_local
    vocab_ids = lax.broadcasted_iota(jnp.int32, logits.shape, 1) + first_vocab
    hits = (vocab_ids == flat_targets[:, None]).astype(jnp.float32)
    grads = probs - hits + entropy_weight * probs * (logits - log_total[:, None] + entropy[:, None])
    projected = jnp.dot(grads.astype(jnp.bfloat16), out_factor, preferred_element_type=jnp.float32)
    group_side = lax.psum_scatter(projected, "dp", scatter_dimension=0, tiled=True)
    out_side = lax.psum_scatter(group_side, "vocab", scatter_dimension=1, tiled=True)
    out_tokens = out_side.reshape(sel_count, token_count, rank_local)
    in_tokens = input_side.reshape(sel_count, token_count, rank_full)
    features = jnp.einsum("etr,etc->erc", out_tokens, in_tokens, precision=lax.Precision.HIGHEST)
    features = features.reshape(sel_count, rank_local * rank_full).astype(jnp.bfloat16)
    gram_rows = row_products(features, lax.all_gather(features, "dp", axis=0, tiled=True))
    return lax.psum_scatter(gram_rows, "vocab", scatter_dimension=1, tiled=True)


def solution(mesh):
    placed = (
        P("dp", None),
        P("dp", None),
        P(),
        P(("dp", "vocab"), None),
        P(("dp", "vocab"), None),
        P("vocab", None),
    )
    return jax.shard_map(
        shards, mesh=mesh, in_specs=placed, out_specs=P("dp", "vocab"), check_vma=False
    )
```

profile of v0, /device:TPU:1, one launch (start us, length us, event | category | flops | bytes accessed | tf_op | source)
XLA Modules:
  0.0 756.4 jit_solution(5228808738773058476)
XLA Ops:
  6.5 0.0 copy-start
  6.5 0.0 all-gather.3.cloned.1.call-start
  6.5 0.9 reshape.52
  7.4 0.8 reshape.51
  8.2 0.0 copy-start.2
  8.3 2.5 gather_fusion
  10.8 0.8 broadcast_select_fusion
  11.6 0.0 all-gather.3.cloned.1.call-update
  11.6 0.0 reduce-scatter.4.cloned.1.call-start
  11.7 0.0 copy-done.2
  11.7 0.1 copy.10
  11.8 0.1 eq.10
  11.9 161.1 %all-gather.3.cloned.1.call-done = bf16[1024,5120]{1,0:T(8,128)(2,1)} async-done(((bf16[32,5120]{1,0:T(8,128)(2,1)}), bf16[1024,5120]{1,0:T(8,128)(2,1)}) %all-gather.3.cloned.1.call-update) | async-done | bytes 10485776 | tf_op jit(solution)/shard_map/all_gather | solution.py:33
  173.0 0.0 copy-done
  173.0 7.1 fusion.10
  180.1 0.0 copy-start.3
  180.1 112.1 %pmax.7 = f32[1024]{0:T(1024)S(1)} all-reduce(f32[1024]{0:T(1024)S(1)} %get-tuple-element.13), channel_id=1, replica_groups=mesh['dp'=32,'vocab'=16] {'dp','vocab'}, use_global_device_ids=true, to_apply=%region_1.2 | all-reduce | flops 1024 | bytes 8192 | tf_op jit(solution)/shard_map/pmax | solution.py:34
  292.2 1.5 fusion
  293.8 94.7 %all-reduce.2 = (f32[1024]{0:T(1024)S(1)}, f32[1024]{0:T(1024)S(1)}) all-reduce(f32[1024]{0:T(1024)S(1)} %get-tuple-element.6, f32[1024]{0:T(1024)S(1)} %get-tuple-element.5), channel_id=1, replica_groups=mesh['dp'=32,'vocab'=16] {'dp','vocab'}, use_global_device_ids=true, to_apply=%region_5.6 | all-reduce | flops 2048 | bytes 16384 | tf_op jit(solution)/shard_map/psum | solution.py:36
  388.5 0.0 copy-done.3
  388.5 0.0 copy-start.1
  388.5 2.9 fusion.1
  391.3 0.0 reduce-scatter.4.cloned.1.call-update
  391.4 1.3 dynamic-slice
  393.9 0.0 copy-done.1
  394.0 1.0 fusion.2
  394.9 126.2 %reduce-scatter.4.cloned.1.call-done = f32[32,128]{1,0:T(8,128)} async-done(((f32[1024,128]{1,0:T(8,128)}), f32[32,128]{1,0:T(8,128)}) %reduce-scatter.4.cloned.1.call-update) | async-done | bytes 16400 | tf_op jit(solution)/shard_map/reduce_scatter | solution.py:47
  521.1 102.0 %all-reduce.3 = (f32[32,128]{1,0:T(8,128)S(1)}, f32[2,16,128]{2,1,0:T(8,128)S(1)}) all-reduce(f32[32,128]{1,0:T(8,128)} %reduce-scatter.4.cloned.1.call-done, f32[2,16,128]{2,1,0:T(8,128)S(1)} %bitcast.20), channel_id=3, replica_groups=mesh['dp'=32,'vocab'=16] {'vocab'}, use_global_device_ids=true, to_apply=%region_7.8.clone | all-reduce | flops 8192 | bytes 65536
  623.2 0.1 constant_dynamic-slice_fusion.1
  623.2 0.2 convolution_convert_fusion
  623.5 61.1 %all-gather = bf16[32,2,1024]{2,1,0:T(2,128)(2,1)S(1)} all-gather(bf16[1,2,1024]{2,1,0:T(2,128)(2,1)S(1)} %reshape.63), channel_id=1, replica_groups=mesh['dp'=32,'vocab'=16] {'dp'}, dimensions={0}, use_global_device_ids=true | all-gather | bytes 135168 | tf_op jit(solution)/shard_map/all_gather | solution.py:53
  684.6 0.1 reshape.64
  684.6 0.1 fusion.4
  684.8 64.1 %all-reduce.1 = f32[2,64]{1,0:T(2,128)S(1)} all-reduce(f32[2,64]{1,0:T(2,128)S(1)} %fusion.4), channel_id=4, replica_groups=mesh['dp'=32,'vocab'=16] {'vocab'}, use_global_device_ids=true, to_apply=%region_9.10.clone | all-reduce | flops 128 | bytes 1024
  748.9 0.6 constant_dynamic-slice_fusion
  (6 shorter events, 0.0 us)
Async XLA Ops:
  6.5 166.5 %copy-start = (bf16[296,5120]{1,0:T(8,128)(2,1)S(1)}, bf16[296,5120]{1,0:T(8,128)(2,1)}, u32[]{:S(2)}) copy-start(bf16[296,5120]{1,0:T(8,128)(2,1)} %param.9) | copy-start | bytes 9093124
  6.5 166.5 %all-gather.3.cloned.1.call-start = ((), (), s32[]{:S(2)}) async-start(), calls=%async_computation.1 | async-start | bytes 10813440 | tf_op jit(solution)/shard_map/all_gather | solution.py:33
  8.2 3.5 copy-start.2
  11.6 509.5 %reduce-scatter.4.cloned.1.call-start = ((), (), s32[]{:S(2)}) async-start(), calls=%async_computation.2 | async-start | bytes 540672 | tf_op jit(solution)/shard_map/reduce_scatter | solution.py:47
  180.1 208.3 %copy-start.3 = (bf16[296,128]{1,0:T(8,128)(2,1)S(1)}, bf16[296,128]{1,0:T(8,128)(2,1)}, u32[]{:S(2)}) copy-start(bf16[296,128]{1,0:T(8,128)(2,1)} %param.10) | copy-start | bytes 227332
  388.5 5.5 copy-start.1
Sparse Core Ops, SparseCore 0:
  11.8 161.1 all-gather.2
  391.5 129.5 reduce-scatter.3
where the time goes:
time: 757 us; the launch traced here: 756 us
  blocking collectives  434 us (57%)
  waiting for transfers between devices  287 us (38%)
  between operations  14.8 us (2%)
  matrix products  11.3 us (1%)
    unnamed x2, blocking collectives  166 us
    all_gather x1, waiting for transfers between devices, shards(): lax.all_gather(selected, 'dp', axis=0, tiled=True)  161 us
    reduce_scatter x1, waiting for transfers between devices, shards(): lax.psum_scatter(projected, 'dp', scatter_dimension=0, tiled=True)  126 us
    pmax x1, blocking collectives, shards(): total_max = lax.pmax(jnp.max(logits, axis=1), ('dp', 'vocab'))  112 us
    psum x1, blocking collectives, shards(): lax.psum((jnp.sum(shifted, axis=1), jnp.sum(shifted * logits, axis=1)), (...  94.7 us
    all_gather x1, blocking collectives, shards(): lax.all_gather(features, 'dp', axis=0, tiled=True)  61.1 us
  transfers between devices with their start and end apart: 2, of which 2 were waited for; matrix products, arithmetic and copies ran while one was open for 0% of the time, Pallas kernels for 0%

commit v1 on v0

v1 whole, which is shorter than its diff:
```python
import jax
import jax.numpy as jnp
from jax import lax
from jax.experimental import pallas as pl
from jax.experimental.pallas import tpu as pltpu
from jax.sharding import PartitionSpec as P

entropy_weight = 0.2
MESH = pl.DeviceIdType.MESH
NX, NY, NZ, NL = 4, 8, 8, 4
F32, BF16 = jnp.float32, jnp.bfloat16
NT = (((1,), (1,)), ((), ()))
TN = (((0,), (0,)), ((), ()))

DIRECT, QUARTER = 1536, 512
WIDE = 2 * DIRECT + QUARTER
HALF_RECT = WIDE // 2
PIECE = HALF_RECT // 2


def device(x, y, z, c):
    return (lax.rem(z, NL) * NY + y, (z // NL) * 2 * NX + x * 2 + c)


def kernel(
    hidden, positions, targets, head, out_factor, in_factor, gram,
    sel, onehot, in_pad, logits, stats, stats_in, proj, core_in, by_rank, x_in, by_y, y_in, own, z_in,
    side, side_in, side_cols, out_own, out_rows, out_cols,
    s_y, s_z, t_z, t_y, x_s, sib_s, st_s, pc_s, px_s, py_s, pz_s, is_s, ix_s, iz_s, id_s, row_s, row_send, col_s, col_send,
):
    dp, v = lax.axis_index("dp"), lax.axis_index("vocab")
    y, zl = lax.rem(dp, NY), dp // NY
    zh, x, c = v // (2 * NX), lax.rem(v, 2 * NX) // 2, lax.rem(v, 2)
    z = zh * NL + zl
    voc_local = head.shape[0]

    def at(dx=0, dy=0, dz=0, dc=0):
        return device(
            lax.rem(x + dx + NX, NX), lax.rem(y + dy + NY, NY), lax.rem(z + dz + NZ, NZ), lax.rem(c + dc, 2)
        )

    x_line = [(dx, dc) for dx in range(NX) for dc in range(2) if dx or dc]
    pending = []

    def copy(src, dst, sent, received, to):
        return pltpu.make_async_remote_copy(
            src_ref=src, dst_ref=dst, send_sem=sent, recv_sem=received, device_id=to, device_id_type=MESH
        )

    def send(src, dst, sems, index, to):
        made = copy(src, dst, sems.at[0, index], sems.at[1, index], to)
        made.start()
        pending.append(made)

    def arrive(dst, sems, index):
        copy(dst, dst, sems.at[0, index], sems.at[1, index], at(dc=1)).wait_recv()

    gives_rows = zl == x
    gives_cols = zh == x // 2
    col_x, col_c = 2 * lax.rem(x, 2) + y // 4, lax.rem(y, 4) // 2
    from_x = zh * 2 + x // 2

    def from_y(i):
        return lax.rem(x, 2) * 4 + c * 2 + i

    own_col = jnp.logical_and(col_x == x, col_c == c)

    barrier = pltpu.get_barrier_semaphore()

    def greet(to):
        pl.semaphore_signal(barrier, inc=1, device_id=to, device_id_type=MESH)

    for dx, dc in x_line:
        greet(at(dx=dx, dc=dc))
    for d in range(1, NY):
        greet(at(dy=d))
        greet(at(dz=d))
    for i in range(2):
        @pl.when(2 * v + i != dp)
        def _():
            greet((2 * v + i, dp // 2))
        for e in range(2):
            @pl.when(jnp.logical_not((from_x == x) & (from_y(i) == y) & (c == e)))
            def _():
                greet(device(from_x, from_y(i), z, e))
    expected = 21 + 2 - (dp // 2 == v).astype(jnp.int32)
    expected += jnp.where(gives_cols, 8 - own_col.astype(jnp.int32), 0)

    place = jnp.concatenate(
        [positions[0:1, :], positions[1:2, :], jnp.full((1, 96), -1, jnp.int32)], axis=1
    )
    hot = (lax.broadcasted_iota(jnp.int32, (128, 128), 0) == place).astype(F32)
    onehot[...] = jnp.transpose(hot)[0:32].astype(BF16)
    mine = onehot[pl.ds(pl.multiple_of(c * 16, 16), 16), :]

    def quarter_of(d):
        return 2 * DIRECT + QUARTER * lax.rem(x - d + NX, NX)

    def whole_column(j):
        j = jnp.asarray(j, jnp.int32)
        start = jnp.where(
            j < 3, j * 512, jnp.where(j == 3, quarter_of(0), jnp.where(j < 7, j * 512 - 512, quarter_of(j - 6)))
        )
        return pl.ds(pl.multiple_of(start, 512), 512)

    for j in range(7):
        sel[c, y, zl, :, 512 * j : 512 * j + 512] = jnp.dot(
            mine, hidden[:, whole_column(j)], preferred_element_type=F32
        ).astype(BF16)

    pl.semaphore_wait(barrier, expected)

    def group(dy):
        return lax.rem(y + dy + NY, NY)

    def plane(dz):
        return lax.rem(zl + dz + NL, NL)

    def cols(start, size):
        return pl.ds(start, size)

    def s_piece(dy, dz, start=0, size=HALF_RECT):
        return sel.at[c, group(dy), plane(dz), :, cols(start, size)]

    def t_piece(dz, start=0, size=HALF_RECT):
        return sel.at[c, y, plane(dz), :, cols(HALF_RECT + start, size)]

    def t_block(dy, start=0, size=HALF_RECT):
        return sel.at[c, group(dy), :, :, cols(HALF_RECT + start, size)]

    def y_index(dy):
        return dy - 1 if dy > 0 else 3 - dy

    def y_part(dy):
        return (0, PIECE) if dy == -4 else (PIECE, PIECE) if dy == 4 else (0, HALF_RECT)

    def forward(k, block, sems):
        if k < 4:
            for dy, step in ((-k, 1), (k, -1)):
                part = y_part(dy - step)
                send(block(dy, *part), block(dy, *part), sems, y_index(dy - step), at(dy=step))

    def s_block(dy, start=0, size=HALF_RECT):
        return s_piece(dy, 0, start, size)

    def arrived(k, block, sems):
        for dy in (-k, k):
            arrive(block(dy, *y_part(dy)), sems, y_index(dy))

    z_moves = ((1, 0, HALF_RECT), (-1, 0, HALF_RECT), (2, 0, PIECE), (-2, PIECE, PIECE))

    def s_z_sends(dy):
        for n, (dz, start, size) in enumerate(z_moves):
            send(s_piece(dy, 0, start, size), s_piece(dy, 0, start, size), s_z, 4 * (dy % 8) + n, at(dz=dz))

    def s_z_arrive(dy):
        for n, (dz, start, size) in enumerate(z_moves):
            arrive(s_piece(dy, -dz, start, size), s_z, 4 * (dy % 8) + n)

    def pair(k):
        return (0,) if k == 0 else (4,) if k == 4 else (k, -k)

    def x_and_sibling(dy):
        for d in range(1, NX):
            send(
                sel.at[c, group(dy), :, :, cols(DIRECT, QUARTER)],
                sel.at[c, group(dy), :, :, cols(WIDE + QUARTER * (d - 1), QUARTER)],
                x_s, 3 * (dy % 8) + d - 1, at(dx=d),
            )
        block = sel.at[c, group(dy), :, :, cols(0, WIDE)]
        send(block, block, sib_s, 2 * (dy % 8), at(dc=1))

    def x_arrive(dy):
        for d in range(1, NX):
            arrive(sel.at[c, group(dy), :, :, cols(WIDE + QUARTER * (d - 1), QUARTER)], x_s, 3 * (dy % 8) + d - 1)
        block = sel.at[c, group(dy), :, :, cols(WIDE, 3 * QUARTER)]
        send(block, block, sib_s, 2 * (dy % 8) + 1, at(dc=1))

    def compute(k):
        dys = pair(k)
        for dy in dys:
            arrive(sel.at[1 - c, group(dy), :, :, cols(0, WIDE)], sib_s, 2 * (dy % 8))
            arrive(sel.at[1 - c, group(dy), :, :, cols(WIDE, 3 * QUARTER)], sib_s, 2 * (dy % 8) + 1)

        def part(j, total):
            where = pl.ds(pl.multiple_of(512 * j, 512), 512)
            rows = [
                sel[e, group(dy), :, :, where].reshape(64, 512) for dy in dys for e in range(2)
            ]
            return total + lax.dot_general(
                head[:, whole_column(j)], jnp.concatenate(rows, axis=0), NT, preferred_element_type=F32
            )

        total = lax.fori_loop(0, 10, part, jnp.zeros((voc_local, 128 * len(dys)), F32))
        for n, dy in enumerate(dys):
            values = total[:, 128 * n : 128 * n + 128]
            row = pl.ds(group(dy), 1)
            top = jnp.max(values, axis=0, keepdims=True)
            lowered = values - top
            power = jnp.exp(lowered)
            logits[group(dy)] = values
            stats[0, 0, row, :] = top
            stats[0, 1, row, :] = jnp.sum(power, axis=0, keepdims=True)
            stats[0, 2, row, :] = jnp.sum(power * lowered, axis=0, keepdims=True)

    def to_cols(i):
        there = lax.rem(dp, 2)
        return copy(side.at[3], side_cols.at[there], id_s.at[0, i], id_s.at[1, there], (2 * v + i, dp // 2))

    forward(0, s_block, s_y)
    for n, (dz, start, size) in enumerate(z_moves):
        send(t_piece(0, start, size), t_piece(0, start, size), t_z, n, at(dz=dz))
    s_z_sends(0)

    window = pl.multiple_of(v * 320 - 64 * c, 128)
    in_pad[...] = jnp.zeros_like(in_pad)
    in_pad[pl.ds(pl.multiple_of(64 * c, 64), 320), :] = in_factor[...]
    chosen = jnp.dot(onehot[...], hidden[:, pl.ds(window, 384)], preferred_element_type=F32).astype(BF16)
    side[0] = jnp.dot(chosen, in_pad[...], preferred_element_type=F32)
    send(side.at[0], side_in.at[0], is_s, 0, at(dc=1))

    for n, (dz, start, size) in enumerate(z_moves):
        arrive(t_piece(-dz, start, size), t_z, n)
    forward(0, t_block, t_y)

    arrive(side_in.at[0], is_s, 0)
    side[1] = side[0] + side_in[0]
    for d in range(1, NX):
        send(side.at[1], side_in.at[d], ix_s, d - 1, at(dx=d))

    for k in range(1, 5):
        arrived(k, s_block, s_y)
        forward(k, s_block, s_y)
        for dy in pair(k):
            s_z_sends(dy)
        for dy in pair(k - 1):
            s_z_arrive(dy)
            x_and_sibling(dy)
        if k == 1:
            for d in range(1, NX):
                arrive(side_in.at[d], ix_s, d - 1)
            side[2] = side[1] + side_in[1] + side_in[2] + side_in[3]
            send(side.at[2], side_in.at[4], iz_s, 0, at(dz=4))
        if k == 2:
            arrive(side_in.at[4], iz_s, 0)
            side[3] = side[2] + side_in[4]
            for i in range(2):
                @pl.when(2 * v + i == dp)
                def _():
                    side_cols[i] = side[3]

                @pl.when(2 * v + i != dp)
                def _():
                    to_cols(i).start()
        arrived(k, t_block, t_y)
        forward(k, t_block, t_y)
        if k >= 2:
            for dy in pair(k - 2):
                x_arrive(dy)
        if k >= 3:
            compute(k - 3)
    x_arrive(3)
    x_arrive(-3)
    s_z_arrive(4)
    x_and_sibling(4)
    compute(2)
    compute(3)
    x_arrive(4)
    compute(4)

    def merge(stage, peers):
        for n, to in enumerate(peers):
            send(stats.at[stage], stats_in.at[stage, n], st_s, 7 * stage + n, to)
        for n in range(7):
            arrive(stats_in.at[stage, n], st_s, 7 * stage + n)
        parts = [stats[stage]] + [stats_in[stage, n] for n in range(7)]
        top = parts[0][0]
        for part in parts[1:]:
            top = jnp.maximum(top, part[0])
        total, weighted = jnp.zeros_like(top), jnp.zeros_like(top)
        for part in parts:
            lower = part[0] - top
            scale = jnp.exp(lower)
            total += scale * part[1]
            weighted += scale * (part[2] + lower * part[1])
        stats[stage + 1, 0] = top
        stats[stage + 1, 1] = total
        stats[stage + 1, 2] = weighted

    merge(0, [at(dx=dx, dc=dc) for dx, dc in x_line])
    merge(1, [at(dy=d) for d in range(1, NY)])
    merge(2, [at(dz=d) for d in range(1, NZ)])
    log_sum = jnp.log(stats[3, 1])
    log_total = stats[3, 0] + log_sum
    entropy = log_sum - stats[3, 2] / stats[3, 1]

    wanted = jnp.concatenate(
        [targets[pl.ds(16 * b + e, 8, stride=2), :] for e in range(2) for b in range(NL)], axis=1
    )
    ids = lax.broadcasted_iota(jnp.int32, (voc_local, 128), 0) + (dp * 2 * NX * 2 + v) * voc_local
    for g in range(NY):
        lowered = logits[g] - log_total[g : g + 1, :]
        probs = jnp.exp(lowered)
        hits = (ids == wanted[g : g + 1, :]).astype(F32)
        grads = probs - hits + entropy_weight * probs * (lowered + entropy[g : g + 1, :])
        result = lax.dot_general(grads.astype(BF16), out_factor[...], TN, preferred_element_type=F32)
        proj[:, :, g] = result.reshape(2, NL, 16, 128)

    send(proj.at[1 - c], core_in, pc_s, 0, at(dc=1))
    arrive(core_in, pc_s, 0)
    by_rank[...] = proj[c] + core_in[...]
    for d in range(1, NX):
        send(by_rank.at[lax.rem(x + d, NX)], x_in.at[d - 1], px_s, d - 1, at(dx=d))
    for d in range(1, NX):
        arrive(x_in.at[d - 1], px_s, d - 1)
    by_y[...] = by_rank[x] + x_in[0] + x_in[1] + x_in[2]
    for d in range(1, NY):
        send(by_y.at[lax.rem(y + d, NY)], y_in.at[d - 1], py_s, d - 1, at(dy=d))
    for d in range(1, NY):
        arrive(y_in.at[d - 1], py_s, d - 1)
    own[...] = by_y[y] + jnp.sum(y_in[...], axis=0)
    for d in range(1, NZ):
        send(own, z_in.at[d - 1], pz_s, d - 1, at(dz=d))
    for d in range(1, NZ):
        arrive(z_in.at[d - 1], pz_s, d - 1)
    out_own[...] = own[...] + jnp.sum(z_in[...], axis=0)

    def row_copy(n):
        dx, dc = x_line[n]
        return copy(out_own, out_rows.at[c], row_send.at[n], row_s.at[c], at(dx=dx, dc=dc))

    slot = lax.rem(y, 2) * 2 + c

    def col_copy(d):
        to = device(col_x, lax.rem(y + d, NY), z, col_c)
        return copy(out_own, out_cols.at[slot], col_send.at[d], col_s.at[slot], to)

    @pl.when(gives_rows)
    def _():
        out_rows[c] = out_own[...]
        for n in range(7):
            row_copy(n).start()

    @pl.when(gives_cols & own_col)
    def _():
        out_cols[slot] = out_own[...]

    @pl.when(gives_cols & jnp.logical_not(own_col))
    def _():
        col_copy(0).start()

    @pl.when(gives_cols)
    def _():
        for d in range(1, NY):
            col_copy(d).start()

    for i in range(2):
        @pl.when(2 * v + i != dp)
        def _():
            copy(side_cols.at[i], side_cols.at[i], id_s.at[0, i], id_s.at[1, i], at(dc=1)).wait_recv()
            to_cols(i).wait_send()

    for e in range(2):
        @pl.when(jnp.logical_not(gives_rows & (c == e)))
        def _():
            copy(out_rows.at[e], out_rows.at[e], row_send.at[0], row_s.at[e], at(dc=1)).wait_recv()
        for i in range(2):
            @pl.when(jnp.logical_not((from_x == x) & (from_y(i) == y) & (c == e)))
            def _():
                n = 2 * i + e
                copy(out_cols.at[n], out_cols.at[n], col_send.at[0], col_s.at[n], at(dc=1)).wait_recv()

    high = lax.Precision.HIGHEST
    outs = lax.dot_general(
        out_rows[...].reshape(32, 128), out_cols[...].reshape(64, 128), NT, precision=high, preferred_element_type=F32
    )
    ins = lax.dot_general(
        side[3], side_cols[...].reshape(64, 128), NT, precision=high, preferred_element_type=F32
    )
    both = outs * ins
    sums = jnp.concatenate(
        [jnp.sum(both[16 * e : 16 * e + 16], axis=0, keepdims=True) for e in range(2)], axis=0
    )
    gram[...] = jnp.concatenate(
        [jnp.sum(sums[:, 16 * f : 16 * f + 16], axis=1, keepdims=True) for f in range(4)], axis=1
    )

    for made in pending:
        made.wait_send()

    @pl.when(gives_rows)
    def _():
        for n in range(7):
            row_copy(n).wait_send()

    @pl.when(gives_cols & jnp.logical_not(own_col))
    def _():
        col_copy(0).wait_send()

    @pl.when(gives_cols)
    def _():
        for d in range(1, NY):
            col_copy(d).wait_send()


def shards(hidden_states, positions, target_ids, head, out_factor, in_factor):
    voc_local, width = head.shape
    rank = out_factor.shape[1]

    def sems(*shape):
        return pltpu.SemaphoreType.DMA(shape)

    return pl.pallas_call(
        kernel,
        out_shape=jax.ShapeDtypeStruct((2, 4), F32),
        in_specs=[pl.BlockSpec(memory_space=pltpu.VMEM)] * 6,
        out_specs=pl.BlockSpec(memory_space=pltpu.VMEM),
        scratch_shapes=[
            pltpu.VMEM((2, NY, NL, 16, width), BF16),
            pltpu.VMEM((32, 128), BF16),
            pltpu.VMEM((384, rank), BF16),
            pltpu.VMEM((NY, voc_local, 128), F32),
            pltpu.VMEM((4, 3, 8, 128), F32),
            pltpu.VMEM((3, 7, 3, 8, 128), F32),
            pltpu.VMEM((2, NL, NY, 16, rank), F32),
            pltpu.VMEM((NL, NY, 16, rank), F32),
            pltpu.VMEM((NL, NY, 16, rank), F32),
            pltpu.VMEM((NX - 1, NY, 16, rank), F32),
            pltpu.VMEM((NY, 16, rank), F32),
            pltpu.VMEM((NY - 1, 16, rank), F32),
            pltpu.VMEM((16, rank), F32),
            pltpu.VMEM((NZ - 1, 16, rank), F32),
            pltpu.VMEM((4, 32, rank), F32),
            pltpu.VMEM((5, 32, rank), F32),
            pltpu.VMEM((2, 32, rank), F32),
            pltpu.VMEM((16, rank), F32),
            pltpu.VMEM((2, 16, rank), F32),
            pltpu.VMEM((4, 16, rank), F32),
            sems(2, 8), sems(2, 32), sems(2, 4), sems(2, 8), sems(2, 24), sems(2, 16), sems(2, 21),
            sems(2, 1), sems(2, 3), sems(2, 7), sems(2, 7), sems(2, 1), sems(2, 3), sems(2, 1), sems(2, 2),
            sems(2), sems(7), sems(4), sems(8),
        ],
        compiler_params=pltpu.CompilerParams(
            collective_id=0, has_side_effects=True, vmem_limit_bytes=48 * 1024 * 1024
        ),
        cost_estimate=pl.CostEstimate(flops=4 * 10**9, bytes_accessed=5 * 10**6, transcendentals=10**6),
    )(hidden_states, positions, target_ids, head, out_factor, in_factor)


def solution(mesh):
    placed = (
        P("dp", None),
        P("dp", None),
        P(),
        P(("dp", "vocab"), None),
        P(("dp", "vocab"), None),
        P("vocab", None),
    )
    return jax.shard_map(
        shards, mesh=mesh, in_specs=placed, out_specs=P("dp", "vocab"), check_vma=False
    )
```

time: 757 us -> 107 us (0.14)
  blocking collectives: 434 us -> 0 us
  waiting for transfers between devices: 287 us -> 0 us
  Pallas kernels: 0 us -> 98.6 us
  between operations: 14.8 us -> 0.01 us
  matrix products: 11.3 us -> 0 us
    unnamed x2 -> x0, blocking collectives: 166 us -> none
    all_gather x1 -> x0, waiting for transfers between devices: 161 us -> none  [shards(): lax.all_gather(selected, 'dp', axis=0, tiled=True)]
    reduce_scatter x1 -> x0, waiting for transfers between devices: 126 us -> none  [shards(): lax.psum_scatter(projected, 'dp', scatter_dimension=0, tiled=True)]
    pmax x1 -> x0, blocking collectives: 112 us -> none  [shards(): total_max = lax.pmax(jnp.max(logits, axis=1), ('dp', 'vocab'))]
    pallas_call x0 -> x1, Pallas kernels: none -> 98.6 us  [shards(): pl.pallas_call(kernel, out_shape=jax.ShapeDtypeStruct((2, 4), F32), in_sp...]
    psum x1 -> x0, blocking collectives: 94.7 us -> none  [shards(): lax.psum((jnp.sum(shifted, axis=1), jnp.sum(shifted * logits, axis=1)), (...]
    all_gather x1 -> x0, blocking collectives: 61.1 us -> none  [shards(): lax.all_gather(features, 'dp', axis=0, tiled=True)]
    dot_general x5 -> x0, matrix products: 11.3 us -> none  [the longest x2 7.27 us: row_products(): lax.dot_general(left_rows, right_rows, (((1,), (1,)), ((), ())), preferre...]
  transfers between devices with their start and end apart: 2 -> 0, of which waited for: 2 -> 0; matrix products, arithmetic and copies ran while one was open for 0% -> 0% of each run, Pallas kernels for 0% -> 0%
where the time goes in v1:
time: 107 us; the launch traced here: 106 us
  Pallas kernels  98.6 us (92%)
  local copies, waits for them, and re-layouts  6.97 us (7%)
    pallas_call x1, Pallas kernels, shards(): pl.pallas_call(kernel, out_shape=jax.ShapeDtypeStruct((2, 4), F32), in_sp...  98.6 us
    unnamed x12, local copies, waits for them, and re-layouts  6.97 us

profile of v1, /device:TPU:1, one launch (start us, length us, event | category | flops | bytes accessed | tf_op | source)
XLA Modules:
  0.0 105.6 jit_solution(12671387150022877806)
XLA Ops:
  0.0 0.8 copy.7.targets
  0.8 0.0 copy-start
  0.8 1.9 %copy-done = bf16[296,5120]{1,0:T(8,128)(2,1)S(1)} copy-done((bf16[296,5120]{1,0:T(8,128)(2,1)S(1)}, bf16[296,5120]{1,0:T(8,128)(2,1)}, u32[]{:S(2)}) %copy-start) | copy-done | bytes 3031064
  2.6 0.0 copy-start.1
  2.6 1.3 %copy-done.1 = bf16[128,5120]{1,0:T(8,128)(2,1)S(1)} copy-done((bf16[128,5120]{1,0:T(8,128)(2,1)S(1)}, bf16[128,5120]{1,0:T(8,128)(2,1)}, u32[]{:S(2)}) %copy-start.1) | copy-done | bytes 1310744
  4.0 0.0 copy-start.2
  4.0 0.9 copy-done.2
  4.8 0.0 copy-start.3
  4.8 0.9 copy-done.3
  5.7 0.0 copy-start.4
  5.7 0.7 copy-done.4
  6.4 98.6 %shard_map.64 = f32[2,4]{1,0:T(2,128)S(1)} custom-call(bf16[128,5120]{1,0:T(8,128)(2,1)S(1)} %copy-done.1, s32[2,16]{1,0:T(2,128)S(1)} %copy-done.4, s32[64,16]{1,0:T(8,128)S(1)} %copy.7.targets, bf16[296,5120]{1,0:T(8,128)(2,1)S(1)} %copy-done, bf16[296,128]{1,0:T(8,128)(2,1)S(1)} %copy-done.3, bf16[320,128]{1,0:T(8,128)(2,1)S(1)} %copy-done.2), custom_call_target="tpu_custom_call" | custom-call | flops 4000000000 | bytes 5000000 | tf_op jit(solution)/shard_map/pallas_call | solution.py:413
  105.0 0.6 copy.9
Async XLA Ops:
  0.8 1.9 %copy-start = (bf16[296,5120]{1,0:T(8,128)(2,1)S(1)}, bf16[296,5120]{1,0:T(8,128)(2,1)}, u32[]{:S(2)}) copy-start(bf16[296,5120]{1,0:T(8,128)(2,1)} %head.1) | copy-start | bytes 9093124
  2.6 1.3 %copy-start.1 = (bf16[128,5120]{1,0:T(8,128)(2,1)S(1)}, bf16[128,5120]{1,0:T(8,128)(2,1)}, u32[]{:S(2)}) copy-start(bf16[128,5120]{1,0:T(8,128)(2,1)} %hidden.1) | copy-start | bytes 3932164
  4.0 0.9 copy-start.2
  4.8 0.9 copy-start.3
  5.7 0.7 copy-start.4

commit v2 on v1

v2 whole, which is shorter than its diff:
```python
import jax
import jax.numpy as jnp
from jax import lax
from jax.experimental import pallas as pl
from jax.experimental.pallas import tpu as pltpu
from jax.sharding import PartitionSpec as P

entropy_weight = 0.2
MESH = pl.DeviceIdType.MESH
NX, NY, NZ, NL = 4, 8, 8, 4
FAR_FIRST = (4, 3, 5, 2, 6, 1, 7)
F32, BF16 = jnp.float32, jnp.bfloat16
NT = (((1,), (1,)), ((), ()))
TN = (((0,), (0,)), ((), ()))

QUARTER, S_DIRECT, T_DIRECT = 512, 1280, 1792
S_WIDE, WIDE = S_DIRECT + QUARTER, S_DIRECT + QUARTER + T_DIRECT
S_HALVES = ((0, S_WIDE // 256 * 128), (S_WIDE // 256 * 128, S_WIDE - S_WIDE // 256 * 128))
T_HALVES = ((0, T_DIRECT // 256 * 128), (T_DIRECT // 256 * 128, T_DIRECT - T_DIRECT // 256 * 128))


def device(x, y, z, c):
    return (lax.rem(z, NL) * NY + y, (z // NL) * 2 * NX + x * 2 + c)


def kernel(
    hidden_hbm, positions, targets, head_hbm, out_factor_hbm, in_factor_hbm, gram,
    hidden, head, out_factor, in_factor, by_example, sel, onehot, in_pad, logits, stats, packed, stats_in, by_rank, x_in, by_y, y_in, own, z_in,
    side, side_in, side_cols, out_own, out_rows, out_cols,
    s_y, o_y, s_z, t_z, t_y, x_s, sib_s, st_s, px_s, py_s, pz_s, is_s, ix_s, iz_s, id_s, row_s, row_send, col_s, col_send, load_s,
):
    dp, v = lax.axis_index("dp"), lax.axis_index("vocab")
    y, zl = lax.rem(dp, NY), dp // NY
    zh, x, c = v // (2 * NX), lax.rem(v, 2 * NX) // 2, lax.rem(v, 2)
    z = zh * NL + zl
    voc_local = head.shape[1]

    def at(dx=0, dy=0, dz=0, dc=0):
        return device(
            lax.rem(x + dx + NX, NX), lax.rem(y + dy + NY, NY), lax.rem(z + dz + NZ, NZ), lax.rem(c + dc, 2)
        )

    x_line = [(dx, dc) for dx in range(NX) for dc in range(2) if dx or dc]
    pending = []

    def copy(src, dst, sent, received, to):
        return pltpu.make_async_remote_copy(
            src_ref=src, dst_ref=dst, send_sem=sent, recv_sem=received, device_id=to, device_id_type=MESH
        )

    def send(src, dst, sems, index, to):
        made = copy(src, dst, sems.at[0, index], sems.at[1, index], to)
        made.start()
        pending.append(made)

    def settle():
        for made in pending:
            made.wait_send()
        pending.clear()

    def arrive(dst, sems, index):
        copy(dst, dst, sems.at[0, index], sems.at[1, index], at(dc=1)).wait_recv()

    loads = [
        pltpu.make_async_copy(src, dst, load_s.at[n])
        for n, (src, dst) in enumerate(
            ((hidden_hbm, hidden), (in_factor_hbm, in_factor), (head_hbm, head.at[c]), (out_factor_hbm, out_factor.at[c]))
        )
    ]
    for load in loads:
        load.start()

    gives_rows = zl == x
    gives_cols = zh == x // 2
    col_x, col_c = 2 * lax.rem(x, 2) + y // 4, lax.rem(y, 4) // 2
    from_x = zh * 2 + x // 2

    def from_y(i):
        return lax.rem(x, 2) * 4 + c * 2 + i

    own_col = jnp.logical_and(col_x == x, col_c == c)

    barrier = pltpu.get_barrier_semaphore()

    def greet(to):
        pl.semaphore_signal(barrier, inc=1, device_id=to, device_id_type=MESH)

    for dx, dc in x_line:
        greet(at(dx=dx, dc=dc))
    for d in range(1, NY):
        greet(at(dy=d))
        greet(at(dz=d))
    for i in range(2):
        @pl.when(2 * v + i != dp)
        def _():
            greet((2 * v + i, dp // 2))
        for e in range(2):
            @pl.when(jnp.logical_not((from_x == x) & (from_y(i) == y) & (c == e)))
            def _():
                greet(device(from_x, from_y(i), z, e))
    expected = 21 + 2 - (dp // 2 == v).astype(jnp.int32)
    expected += jnp.where(gives_cols, 8 - own_col.astype(jnp.int32), 0)

    place = jnp.concatenate(
        [positions[0:1, :], positions[1:2, :], jnp.full((1, 96), -1, jnp.int32)], axis=1
    )
    hot = (lax.broadcasted_iota(jnp.int32, (128, 128), 0) == place).astype(F32)
    onehot[...] = jnp.transpose(hot)[0:32].astype(BF16)
    mine = onehot[pl.ds(pl.multiple_of(c * 16, 16), 16), :]

    def quarter_of(d):
        return pl.multiple_of(S_DIRECT + T_DIRECT + QUARTER * lax.rem(x - d + NX, NX), 128)

    runs = [
        (0, S_DIRECT, 0),
        (S_DIRECT, QUARTER, quarter_of(0)),
        (S_WIDE, T_DIRECT, S_DIRECT),
        *[(WIDE + QUARTER * (d - 1), QUARTER, quarter_of(d)) for d in range(1, NX)],
    ]

    loads[0].wait()
    for start, size, whole in runs[:3]:
        sel[y, 0, :, start : start + size] = jnp.dot(
            mine, hidden[:, pl.ds(whole, size)], preferred_element_type=F32
        ).astype(BF16)

    pl.semaphore_wait(barrier, expected)

    def group(dy):
        return lax.rem(y + dy + NY, NY)

    def cols(start, size):
        return pl.ds(start, size)

    def s_piece(dy, dz, start=0, size=S_WIDE):
        return sel.at[group(dy), dz % NL, :, cols(start, size)]

    def t_piece(dz, start=0, size=T_DIRECT):
        return sel.at[y, dz % NL, :, cols(S_WIDE + start, size)]

    def t_block(dy, half):
        return sel.at[group(dy), pl.ds(1, NL - 1), :, cols(S_WIDE + T_HALVES[half][0], T_HALVES[half][1])]

    def y_index(dy):
        return dy - 1 if dy > 0 else 3 - dy

    def s_part(dy):
        return S_HALVES[0] if dy == -4 else S_HALVES[1] if dy == 4 else (0, S_WIDE)

    def s_forward(k):
        for dy, step in ((-k, 1), (k, -1)):
            piece = s_piece(dy, 0, *s_part(dy - step))
            send(piece, piece, s_y, y_index(dy - step), at(dy=step))

    def s_arrived(k):
        for dy in (-k, k):
            arrive(s_piece(dy, 0, *s_part(dy)), s_y, y_index(dy))

    def own_part(dy, part):
        start, size = T_HALVES[0] if part == -4 else T_HALVES[1] if part == 4 else (0, T_DIRECT)
        return sel.at[group(dy), 0, :, cols(S_WIDE + start, size)]

    def own_forward(k):
        for dy, step in ((-k, 1), (k, -1)):
            piece = own_part(dy, dy - step)
            send(piece, piece, o_y, y_index(dy - step), at(dy=step))

    def own_arrived(k):
        for dy in (-k, k):
            arrive(own_part(dy, dy), o_y, y_index(dy))

    def t_forward(k, half):
        for dy, step in ((-k, 1), (k, -1)):
            if k < 3 or half == (step < 0):
                send(t_block(dy, half), t_block(dy, half), t_y, 2 * y_index(dy - step) + half, at(dy=step))

    def t_arrived(k, half):
        for dy in (-k, k):
            if k < 4 or half == (dy > 0):
                arrive(t_block(dy, half), t_y, 2 * y_index(dy) + half)

    def z_moves(halves):
        whole = (0, halves[0][1] + halves[1][1])
        return ((1, *whole), (-1, *whole), (2, *halves[0]), (-2, *halves[1]))

    def s_z_sends(dy):
        for n, (dz, start, size) in enumerate(z_moves(S_HALVES)):
            send(s_piece(dy, 0, start, size), s_piece(dy, -dz, start, size), s_z, 4 * (dy % 8) + n, at(dz=dz))

    def s_z_arrive(dy):
        for n, (dz, start, size) in enumerate(z_moves(S_HALVES)):
            arrive(s_piece(dy, -dz, start, size), s_z, 4 * (dy % 8) + n)

    def pair(k):
        return (0,) if k == 0 else (4,) if k == 4 else (k, -k)

    def x_sends(dy):
        s_z_arrive(dy)
        for d in range(1, NX):
            send(
                sel.at[group(dy), :, :, cols(S_DIRECT, QUARTER)],
                sel.at[group(dy), :, :, cols(WIDE + QUARTER * (d - 1), QUARTER)],
                x_s, 3 * (dy % 8) + d - 1, at(dx=d),
            )

    def x_arrive(dy):
        for d in range(1, NX):
            arrive(sel.at[group(dy), :, :, cols(WIDE + QUARTER * (d - 1), QUARTER)], x_s, 3 * (dy % 8) + d - 1)

    def compute(*dys):
        total = [jnp.zeros((voc_local, 64 * len(dys)), F32) for _ in range(2)]
        for start, size, whole in runs:
            rows = [
                sel[group(dy), lax.rem(p - zl + NL, NL), :, start : start + size] for dy in dys for p in range(NL)
            ]
            rows = jnp.concatenate(rows, axis=0)
            for h in range(2):
                total[h] += lax.dot_general(head[h, :, pl.ds(whole, size)], rows, NT, preferred_element_type=F32)
        for n, dy in enumerate(dys):
            values = [total[h][:, 64 * n : 64 * n + 64] for h in range(2)]
            row = pl.ds(group(dy), 1)
            top = jnp.maximum(*[jnp.max(part, axis=0, keepdims=True) for part in values])
            power_sum, weighted = jnp.zeros_like(top), jnp.zeros_like(top)
            for h in range(2):
                lowered = values[h] - top
                power = jnp.exp(lowered)
                logits[group(dy), h] = values[h]
                power_sum += jnp.sum(power, axis=0, keepdims=True)
                weighted += jnp.sum(power * lowered, axis=0, keepdims=True)
            unused = jnp.ones((1, 64), F32)
            for n_stat, value in enumerate((top, power_sum, weighted)):
                stats[n_stat, row, :] = jnp.concatenate([value, unused], axis=1)

    def to_cols(i):
        there = lax.rem(dp, 2)
        return copy(side.at[3], side_cols.at[there], id_s.at[0, i], id_s.at[1, there], (2 * v + i, dp // 2))

    def t_relay(k, half):
        t_arrived(k, half)
        if k < 4:
            t_forward(k, half)

    s_forward(0)
    for n, (dz, start, size) in enumerate(z_moves(T_HALVES)):
        send(t_piece(0, start, size), t_piece(-dz, start, size), t_z, n, at(dz=dz))
    s_z_sends(0)

    loads[1].wait()
    window = pl.multiple_of(v * 320 - 64 * c, 128)
    in_pad[...] = jnp.zeros_like(in_pad)
    in_pad[pl.ds(pl.multiple_of(64 * c, 64), 320), :] = in_factor[...]
    chosen = jnp.dot(onehot[...], hidden[:, pl.ds(window, 384)], preferred_element_type=F32).astype(BF16)
    side[0] = jnp.dot(chosen, in_pad[...], preferred_element_type=F32)
    send(side.at[0], side_in.at[0], is_s, 0, at(dc=1))

    s_arrived(1)
    s_forward(1)
    own_forward(0)
    for n, (dz, start, size) in enumerate(z_moves(T_HALVES)):
        arrive(t_piece(-dz, start, size), t_z, n)
    t_forward(0, 0)
    s_z_sends(1)
    t_forward(0, 1)
    by_example[...] = jnp.transpose(
        jnp.pad(targets[...], ((0, 112), (0, 64))).astype(F32)
    )[0:64].astype(jnp.int32)
    for load in loads[2:]:
        load.wait()
    send(head.at[c], head.at[c], sib_s, 0, at(dc=1))
    send(out_factor.at[c], out_factor.at[c], sib_s, 1, at(dc=1))
    s_arrived(2)
    s_forward(2)
    own_arrived(1)
    own_forward(1)
    x_sends(0)
    s_z_sends(-1)
    arrive(side_in.at[0], is_s, 0)
    side[1] = side[0] + side_in[0]
    for d in range(1, NX):
        send(side.at[1], side_in.at[d], ix_s, d - 1, at(dx=d))
    t_relay(1, 0)
    s_arrived(3)
    s_forward(3)
    own_arrived(2)
    own_forward(2)
    s_z_sends(2)
    x_sends(1)
    t_relay(1, 1)
    s_arrived(4)
    own_arrived(3)
    own_forward(3)
    s_z_sends(-2)
    x_sends(-1)
    x_arrive(0)
    for d in range(1, NX):
        arrive(side_in.at[d], ix_s, d - 1)
    side[2] = side[1] + side_in[1] + side_in[2] + side_in[3]
    send(side.at[2], side_in.at[4], iz_s, 0, at(dz=4))
    t_relay(2, 0)
    s_z_sends(3)
    x_sends(2)
    x_arrive(1)
    t_relay(2, 1)
    arrive(head.at[1 - c], sib_s, 0)
    arrive(out_factor.at[1 - c], sib_s, 1)
    compute(0, 1)
    s_z_sends(-3)
    x_sends(-2)
    x_arrive(-1)
    arrive(side_in.at[4], iz_s, 0)
    side[3] = side[2] + side_in[4]
    for i in range(2):
        @pl.when(2 * v + i == dp)
        def _():
            side_cols[i] = side[3]

        @pl.when(2 * v + i != dp)
        def _():
            to_cols(i).start()
    t_relay(3, 0)
    s_z_sends(4)
    x_sends(3)
    x_arrive(2)
    t_relay(3, 1)
    x_sends(-3)
    x_arrive(-2)
    own_arrived(4)
    t_relay(4, 0)
    t_relay(4, 1)
    x_sends(4)
    compute(-1, 2)
    x_arrive(3)
    compute(-2, 3)
    x_arrive(-3)
    x_arrive(4)
    compute(-3, 4)

    def pack(*values):
        return jnp.concatenate([*values, jnp.zeros((4, 128), F32)], axis=0)

    packed[0] = pack(
        *[jnp.concatenate([stats[n, 0:4, 0:64], stats[n, 4:8, 0:64]], axis=1) for n in range(3)]
    )

    def merge(stage, peers):
        for n, to in enumerate(peers):
            send(packed.at[stage], stats_in.at[stage, n], st_s, 7 * stage + n, to)
        if stage:
            settle()
        for n in range(len(peers)):
            arrive(stats_in.at[stage, n], st_s, 7 * stage + n)
        parts = [packed[stage]] + [stats_in[stage, n] for n in range(len(peers))]
        top = parts[0][0:4]
        for part in parts[1:]:
            top = jnp.maximum(top, part[0:4])
        total, weighted = jnp.zeros_like(top), jnp.zeros_like(top)
        for part in parts:
            lower = part[0:4] - top
            scale = jnp.exp(lower)
            total += scale * part[4:8]
            weighted += scale * (part[8:12] + lower * part[4:8])
        packed[stage + 1] = pack(top, total, weighted)

    merge(0, [at(dx=d) for d in (2, 1, 3)])
    merge(1, [at(dy=d) for d in FAR_FIRST])
    merge(2, [at(dz=d) for d in FAR_FIRST])
    log_sum = jnp.log(packed[3, 4:8, :])
    log_totals = packed[3, 0:4, :] + log_sum
    entropies = log_sum - packed[3, 8:12, :] / packed[3, 4:8, :]

    wanted = jnp.concatenate(
        [
            jnp.where(c == 0, *[by_example[pl.ds(16 * b + e, 8, stride=2), 0:16] for e in range(2)])
            for b in range(NL)
        ],
        axis=1,
    )
    ids = lax.broadcasted_iota(jnp.int32, (voc_local, 64), 0) + (dp * 2 * NX * 2 + v - c) * voc_local
    for g in range(NY):
        spot = (slice(g % 4, g % 4 + 1), slice(g // 4 * 64, g // 4 * 64 + 64))
        log_total, entropy = log_totals[spot], entropies[spot]
        result = jnp.zeros((64, out_factor.shape[2]), F32)
        for h in range(2):
            lowered = logits[g, h] - log_total
            probs = jnp.exp(lowered)
            hits = (ids + h * voc_local == wanted[g : g + 1, :]).astype(F32)
            grads = probs - hits + entropy_weight * probs * (lowered + entropy)
            result += lax.dot_general(grads.astype(BF16), out_factor[h], TN, preferred_element_type=F32)
        by_rank[:, g] = result.astype(BF16).reshape(NL, 16, 128)

    for d in (2, 1, 3):
        send(by_rank.at[lax.rem(x + d, NX)], x_in.at[d - 1], px_s, d - 1, at(dx=d))
    for d in range(1, NX):
        arrive(x_in.at[d - 1], px_s, d - 1)
    by_y[...] = by_rank[x].astype(F32) + x_in[0].astype(F32) + x_in[1].astype(F32) + x_in[2].astype(F32)
    for d in FAR_FIRST:
        send(by_y.at[lax.rem(y + d, NY)], y_in.at[d - 1], py_s, d - 1, at(dy=d))
    for d in range(1, NY):
        arrive(y_in.at[d - 1], py_s, d - 1)
    own[...] = by_y[y] + jnp.sum(y_in[...], axis=0)
    for d in FAR_FIRST:
        send(own, z_in.at[d - 1], pz_s, d - 1, at(dz=d))
    settle()
    for d in range(1, NZ):
        arrive(z_in.at[d - 1], pz_s, d - 1)
    out_own[...] = own[...] + jnp.sum(z_in[...], axis=0)

    def row_copy(n):
        dx, dc = x_line[n]
        return copy(out_own, out_rows.at[c], row_send.at[n], row_s.at[c], at(dx=dx, dc=dc))

    slot = lax.rem(y, 2) * 2 + c

    def col_copy(d):
        to = device(col_x, lax.rem(y + d, NY), z, col_c)
        return copy(out_own, out_cols.at[slot], col_send.at[d], col_s.at[slot], to)

    @pl.when(gives_cols & own_col)
    def _():
        out_cols[slot] = out_own[...]

    @pl.when(gives_cols & jnp.logical_not(own_col))
    def _():
        col_copy(0).start()

    @pl.when(gives_cols)
    def _():
        for d in FAR_FIRST:
            col_copy(d).start()

    @pl.when(gives_rows)
    def _():
        out_rows[c] = out_own[...]
        for n in range(7):
            row_copy(n).start()

    for i in range(2):
        @pl.when(2 * v + i != dp)
        def _():
            copy(side_cols.at[i], side_cols.at[i], id_s.at[0, i], id_s.at[1, i], at(dc=1)).wait_recv()
            to_cols(i).wait_send()

    settle()
    ins = lax.dot_general(
        side[3], side_cols[...].reshape(64, 128), NT, precision=lax.Precision.HIGHEST, preferred_element_type=F32
    )
    for e in range(2):
        @pl.when(jnp.logical_not(gives_rows & (c == e)))
        def _():
            copy(out_rows.at[e], out_rows.at[e], row_send.at[0], row_s.at[e], at(dc=1)).wait_recv()
        for i in range(2):
            @pl.when(jnp.logical_not((from_x == x) & (from_y(i) == y) & (c == e)))
            def _():
                n = 2 * i + e
                copy(out_cols.at[n], out_cols.at[n], col_send.at[0], col_s.at[n], at(dc=1)).wait_recv()

    high = lax.Precision.HIGHEST
    outs = lax.dot_general(
        out_rows[...].reshape(32, 128), out_cols[...].reshape(64, 128), NT, precision=high, preferred_element_type=F32
    )
    both = outs * ins
    sums = jnp.concatenate(
        [jnp.sum(both[16 * e : 16 * e + 16], axis=0, keepdims=True) for e in range(2)], axis=0
    )
    gram[...] = jnp.concatenate(
        [jnp.sum(sums[:, 16 * f : 16 * f + 16], axis=1, keepdims=True) for f in range(4)], axis=1
    )

    @pl.when(gives_rows)
    def _():
        for n in range(7):
            row_copy(n).wait_send()

    @pl.when(gives_cols & jnp.logical_not(own_col))
    def _():
        col_copy(0).wait_send()

    @pl.when(gives_cols)
    def _():
        for d in range(1, NY):
            col_copy(d).wait_send()


def shards(hidden_states, positions, target_ids, head, out_factor, in_factor):
    voc_local, width = head.shape
    rank = out_factor.shape[1]

    def sems(*shape):
        return pltpu.SemaphoreType.DMA(shape)

    return pl.pallas_call(
        kernel,
        out_shape=jax.ShapeDtypeStruct((2, 4), F32),
        in_specs=[
            pl.BlockSpec(memory_space=space)
            for space in (pltpu.HBM, pltpu.VMEM, pltpu.VMEM, pltpu.HBM, pltpu.HBM, pltpu.HBM)
        ],
        out_specs=pl.BlockSpec(memory_space=pltpu.VMEM),
        scratch_shapes=[
            pltpu.VMEM(hidden_states.shape, BF16),
            pltpu.VMEM((2, *head.shape), BF16),
            pltpu.VMEM((2, *out_factor.shape), BF16),
            pltpu.VMEM(in_factor.shape, BF16),
            pltpu.VMEM((64, 128), jnp.int32),
            pltpu.VMEM((NY, NL, 16, width), BF16),
            pltpu.VMEM((32, 128), BF16),
            pltpu.VMEM((384, rank), BF16),
            pltpu.VMEM((NY, 2, voc_local, 64), F32),
            pltpu.VMEM((3, 8, 128), F32),
            pltpu.VMEM((4, 16, 128), F32),
            pltpu.VMEM((3, 7, 16, 128), F32),
            pltpu.VMEM((NL, NY, 16, rank), BF16),
            pltpu.VMEM((NX - 1, NY, 16, rank), BF16),
            pltpu.VMEM((NY, 16, rank), F32),
            pltpu.VMEM((NY - 1, 16, rank), F32),
            pltpu.VMEM((16, rank), F32),
            pltpu.VMEM((NZ - 1, 16, rank), F32),
            pltpu.VMEM((4, 32, rank), F32),
            pltpu.VMEM((5, 32, rank), F32),
            pltpu.VMEM((2, 32, rank), F32),
            pltpu.VMEM((16, rank), F32),
            pltpu.VMEM((2, 16, rank), F32),
            pltpu.VMEM((4, 16, rank), F32),
            sems(2, 8), sems(2, 8), sems(2, 32), sems(2, 4), sems(2, 16), sems(2, 24), sems(2, 2), sems(2, 21),
            sems(2, 3), sems(2, 7), sems(2, 7), sems(2, 1), sems(2, 3), sems(2, 1), sems(2, 2),
            sems(2), sems(7), sems(4), sems(8), sems(4),
        ],
        compiler_params=pltpu.CompilerParams(
            collective_id=0, has_side_effects=True, vmem_limit_bytes=60 * 1024 * 1024
        ),
        cost_estimate=pl.CostEstimate(flops=4 * 10**9, bytes_accessed=5 * 10**6, transcendentals=10**6),
    )(hidden_states, positions, target_ids.T, head, out_factor, in_factor)


def solution(mesh):
    placed = (
        P("dp", None),
        P("dp", None),
        P(),
        P(("dp", "vocab"), None),
        P(("dp", "vocab"), None),
        P("vocab", None),
    )
    return jax.shard_map(
        shards, mesh=mesh, in_specs=placed, out_specs=P("dp", "vocab"), check_vma=False
    )
```

time: 107 us -> 92.7 us (0.87); the launches traced: 106 us -> 92.5 us
  Pallas kernels: 98.6 us -> 91.3 us
  local copies, waits for them, and re-layouts: 6.97 us -> 1.24 us
    pallas_call x1, Pallas kernels: 98.6 us -> 91.3 us  [shards(): pl.pallas_call(kernel, out_shape=jax.ShapeDtypeStruct((2, 4), F32), in_sp...]
    unnamed x12 -> x1, local copies, waits for them, and re-layouts: 6.97 us -> 1.24 us
where the time goes in v2:
time: 92.7 us; the launch traced here: 92.5 us
  Pallas kernels  91.3 us (98%)
  local copies, waits for them, and re-layouts  1.24 us (1%)
    pallas_call x1, Pallas kernels, shards(): pl.pallas_call(kernel, out_shape=jax.ShapeDtypeStruct((2, 4), F32), in_sp...  91.3 us

profile of v2, /device:TPU:1, one launch (start us, length us, event | category | flops | bytes accessed | tf_op | source)
XLA Modules:
  0.0 92.5 jit_solution(6285456234514740573)
XLA Ops:
  0.0 91.3 %shard_map.64 = f32[2,4]{1,0:T(2,128)} custom-call(bf16[128,5120]{1,0:T(8,128)(2,1)} %hidden_hbm.1, s32[2,16]{1,0:T(2,128)} %positions.1, s32[16,64]{1,0:T(8,128)} %bitcast.1, bf16[296,5120]{1,0:T(8,128)(2,1)} %head_hbm.1, bf16[296,128]{1,0:T(8,128)(2,1)} %out_factor_hbm.1, bf16[320,128]{1,0:T(8,128)(2,1)} %in_factor_hbm.1), custom_call_target="tpu_custom_call" | custom-call | flops 4000000000 | bytes 5000000 | tf_op jit(solution)/shard_map/pallas_call | solution.py:491
  91.3 1.2 %copy.8 = f32[2,4]{1,0:T(2,128)} copy(f32[2,4]{1,0:T(2,128)} %shard_map.64) | data formatting | bytes 64

commit v3 on v2

--- a/solution.py
+++ b/solution.py
@@ -13,7 +13,7 @@
 NT = (((1,), (1,)), ((), ()))
 TN = (((0,), (0,)), ((), ()))
 
-QUARTER, S_DIRECT, T_DIRECT = 512, 1280, 1792
+QUARTER, S_DIRECT, T_DIRECT = 512, 1024, 2048
 S_WIDE, WIDE = S_DIRECT + QUARTER, S_DIRECT + QUARTER + T_DIRECT
 S_HALVES = ((0, S_WIDE // 256 * 128), (S_WIDE // 256 * 128, S_WIDE - S_WIDE // 256 * 128))
 T_HALVES = ((0, T_DIRECT // 256 * 128), (T_DIRECT // 256 * 128, T_DIRECT - T_DIRECT // 256 * 128))

time: 92.7 us -> 93 us (level)
  no operation moved by 1% of the time
where the time goes in v3:
time: 93 us; the launch traced here: 92.8 us
  Pallas kernels  91.6 us (98%)
  local copies, waits for them, and re-layouts  1.24 us (1%)
    pallas_call x1, Pallas kernels, shards(): pl.pallas_call(kernel, out_shape=jax.ShapeDtypeStruct((2, 4), F32), in_sp...  91.6 us

profile of v3, /device:TPU:1, one launch (start us, length us, event | category | flops | bytes accessed | tf_op | source)
XLA Modules:
  0.0 92.8 jit_solution(17265383141887948086)
XLA Ops:
  0.0 91.6 %shard_map.64 = f32[2,4]{1,0:T(2,128)} custom-call(bf16[128,5120]{1,0:T(8,128)(2,1)} %hidden_hbm.1, s32[2,16]{1,0:T(2,128)} %positions.1, s32[16,64]{1,0:T(8,128)} %bitcast.1, bf16[296,5120]{1,0:T(8,128)(2,1)} %head_hbm.1, bf16[296,128]{1,0:T(8,128)(2,1)} %out_factor_hbm.1, bf16[320,128]{1,0:T(8,128)(2,1)} %in_factor_hbm.1), custom_call_target="tpu_custom_call" | custom-call | flops 4000000000 | bytes 5000000 | tf_op jit(solution)/shard_map/pallas_call | solution.py:491
  91.6 1.2 %copy.8 = f32[2,4]{1,0:T(2,128)} copy(f32[2,4]{1,0:T(2,128)} %shard_map.64) | data formatting | bytes 64
